TPU v7x, 128 devices: a whole 4x4x4 slice. The times are simulated.
128 devices in a mesh: dp: 32 (over x, y, core), tensor: 4 (over z).
Axes of the slice: x: 4, y: 4, z: 4, core: 2. Of those that a mesh axis runs over, the one named last changes fastest.
Arguments:
- inputs: bfloat16 [16384, 2048], P(('dp', 'tensor')), may hold values from -6 to 6
- cotangent: bfloat16 [16384, 2048], P(('dp', 'tensor')), may hold values from -6 to 6
- positions: int32 [16384], P('dp'), may hold values from 0 to 511, as said below
- qkv_weight: float32 [2048, 3, 2048], P('dp', None, 'tensor'), may hold values from -0.1875 to 0.1875
- out_weight: float32 [2048, 2048], P('tensor', 'dp'), may hold values from -0.75 to 0.75
- up_weight: float32 [2048, 8192], P('dp', 'tensor'), may hold values from -0.125 to 0.125
- down_weight: float32 [8192, 2048], P('tensor', 'dp'), may hold values from -0.0625 to 0.0625
- qkv_moment: float32 [2048, 3, 2048], P('dp', None, 'tensor'), may hold values from -160 to 160
- out_moment: float32 [2048, 2048], P('tensor', 'dp'), may hold values from -160 to 160
- up_moment: float32 [2048, 8192], P('dp', 'tensor'), may hold values from -192 to 192
- down_moment: float32 [8192, 2048], P('tensor', 'dp'), may hold values from -448 to 448
- vectors: float32 [11, 2048], P(None, ('dp', 'tensor')), may hold values from -0.6 to 1.6, as said below
- vector_first: float32 [11, 2048], P(None, ('dp', 'tensor')), may hold values from -57.6 to 57.6
- vector_second: float32 [11, 2048], P(None, ('dp', 'tensor')), may hold values from 8.192 to 3604.48
Outputs:
- layer_out: bfloat16 [16384, 2048], P(('dp', 'tensor'))
- input_grad: float32 [16384, 2048], P(('dp', 'tensor'))
- qkv_new: float32 [2048, 3, 2048], P('dp', None, 'tensor')
- out_new: float32 [2048, 2048], P('tensor', 'dp')
- up_new: float32 [2048, 8192], P('dp', 'tensor')
- down_new: float32 [8192, 2048], P('tensor', 'dp')
- qkv_moment_new: float32 [2048, 3, 2048], P('dp', None, 'tensor')
- out_moment_new: float32 [2048, 2048], P('tensor', 'dp')
- up_moment_new: float32 [2048, 8192], P('dp', 'tensor')
- down_moment_new: float32 [8192, 2048], P('tensor', 'dp')
- vector_first_new: float32 [11, 2048], P(None, ('dp', 'tensor'))
- vector_second_new: float32 [11, 2048], P(None, ('dp', 'tensor'))
- vectors_new: float32 [11, 2048], P(None, ('dp', 'tensor'))
Inputs may be any that keep to these rules, and one draw needn't show every extreme that they name: `positions`: within each aligned block of 512 tokens, the first has position 0 and every other has the position of the token before it plus one, or 0 where a new sequence starts; in some block all 512 tokens form one sequence. `vectors`: row 0 lies near 1, the other rows near 0.
All inputs are finite; a program needn't handle non-finite values.
Results may differ from a plain program's by a relative error of at most 0.015.
The roundings to bfloat16 on the way count: a program that leaves them out, or rounds other values in their place, can miss the bound.
Values may be sent and summed in bfloat16 or wider, within the bound.
A program may use at most 192 MiB of HBM per device.

v0:
```python
import jax
import jax.numpy as jnp
from jax import lax
from jax.sharding import PartitionSpec as P

HEAD = 64
ROT = 32
BR = 256
SWEEPS = 5
STEP = 10


highest = lax.Precision.HIGHEST
norm_epsilon = 1e-05
ortho_epsilon = 1e-07
masked_score = -1e30
rotary_base = 10000.0
muon_decay = 0.95
coef_linear = 3.4445
coef_square = -4.775
coef_cubic = 2.0315
decay_factor = 0.01
rate_qkv = 1.0
rate_out = 4.0
rate_up = 0.8
rate_down = 0.4
adam_rate = 0.2
first_decay = 0.9
second_decay = 0.95
adam_epsilon = 1e-08


def as_sent(value):

    def short(part):
        return part.astype(jnp.bfloat16) if part.dtype == jnp.float32 else part

    return jax.tree.map(short, value)


def rotary_tables(positions, half_rot):
    freq_index = jnp.arange(half_rot).astype(jnp.float32)
    inverse_freq = rotary_base ** (-2.0 * freq_index / (2 * half_rot))
    angles = positions.astype(jnp.float32)[:, None] * inverse_freq[None, :]
    return (jnp.cos(angles)[:, None, :], jnp.sin(angles)[:, None, :])


def rotate(vectors_in, cosine_table, sine_table, half_rot):
    first_half = vectors_in[..., :half_rot]
    second = vectors_in[..., half_rot : 2 * half_rot]
    remainder = vectors_in[..., 2 * half_rot :]
    return jnp.concatenate(
        [
            first_half * cosine_table - second * sine_table,
            second * cosine_table + first_half * sine_table,
            remainder,
        ],
        -1,
    )


def unrotate(grads_in, cosine_table, sine_table, half_rot):
    first_half = grads_in[..., :half_rot]
    second = grads_in[..., half_rot : 2 * half_rot]
    remainder = grads_in[..., 2 * half_rot :]
    return jnp.concatenate(
        [
            first_half * cosine_table + second * sine_table,
            second * cosine_table - first_half * sine_table,
            remainder,
        ],
        -1,
    )


def gelu_tanh(values):
    return jax.nn.gelu(values, approximate=True)


def score_block(query_block, key_low, positions, row_start, scale_value):
    block_len = query_block.shape[0]
    raw_scores = (
        jnp.einsum("qhe,khe->hqk", query_block, key_low, preferred_element_type=jnp.float32)
        * scale_value
    )
    query_ids = row_start + jnp.arange(block_len)
    key_ids = jnp.arange(key_low.shape[0])
    visible = (key_ids[None, :] <= query_ids[:, None]) & (
        query_ids[:, None] - key_ids[None, :] <= positions[:, None]
    )
    return jnp.where(visible[None], raw_scores, masked_score)


def column_blocks(matrix):
    return matrix.reshape(matrix.shape[0], -1, BR).transpose(1, 2, 0)


def column_restore(blocks, shape):
    return blocks.transpose(2, 0, 1).reshape(shape)


def orthogonalize(blocks):
    norms = jnp.sqrt(jnp.sum(blocks * blocks, axis=(1, 2), keepdims=True))
    current = blocks / (norms + ortho_epsilon)
    for sweep_index in range(SWEEPS):
        gram_matrix = jnp.einsum("bik,bjk->bij", current, current, precision=highest)
        polynomial = coef_square * gram_matrix + coef_cubic * jnp.einsum(
            "bij,bjk->bik", gram_matrix, gram_matrix, precision=highest
        )
        current = coef_linear * current + jnp.einsum(
            "bij,bjk->bik", polynomial, current, precision=highest
        )
    return current


def owner_work(received):
    source_count, item_count, block_rows, piece_width = received.shape
    blocks = received.transpose(1, 2, 0, 3).reshape(
        item_count, block_rows, source_count * piece_width
    )
    orthogonal = orthogonalize(blocks)
    return orthogonal.reshape(item_count, block_rows, source_count, piece_width).transpose(
        2, 0, 1, 3
    )


def local(
    inputs,
    cotangent,
    positions,
    qkv_weight,
    out_weight,
    up_weight,
    down_weight,
    qkv_moment,
    out_moment,
    up_moment,
    down_moment,
    vectors,
    vector_first,
    vector_second,
):
    low_type = jnp.bfloat16
    qkv_full, out_full, up_full, down_full = (
        lax.all_gather(qkv_weight.astype(low_type), "dp", axis=0, tiled=True),
        lax.all_gather(out_weight.astype(low_type), "dp", axis=1, tiled=True),
        lax.all_gather(up_weight.astype(low_type), "dp", axis=0, tiled=True),
        lax.all_gather(down_weight.astype(low_type), "dp", axis=1, tiled=True),
    )
    vector_table = lax.all_gather(vectors, ("dp", "tensor"), axis=1, tiled=True)
    feature_width = vector_table.shape[1]
    head_width = qkv_full.shape[2]
    hidden_width = up_full.shape[1]
    heads_here = head_width // HEAD
    tensor_rank = lax.axis_index("tensor")
    qkv_bias = lax.dynamic_slice_in_dim(vector_table[2:5], tensor_rank * head_width, head_width, 1)
    up_bias = lax.dynamic_slice_in_dim(
        vector_table[7:].reshape(-1), tensor_rank * hidden_width, hidden_width, 0
    )
    norm_gain = vector_table[0]
    norm_shift = vector_table[1]
    residual = inputs.astype(jnp.float32)
    center = residual - jnp.mean(residual, -1, keepdims=True)
    variance = jnp.mean(center * center, -1, keepdims=True)
    scale_inv = lax.rsqrt(variance + norm_epsilon)
    normed = center * scale_inv
    hidden_low = (normed * norm_gain + norm_shift).astype(low_type)
    gathered = lax.all_gather(hidden_low, "tensor", axis=0, tiled=True)
    row_count = gathered.shape[0]
    qkv_lin = (
        jnp.einsum("rd,dcn->rcn", gathered, qkv_full, preferred_element_type=jnp.float32)
        + qkv_bias[None]
    )
    cosine_table, sine_table = rotary_tables(positions, ROT // 2)
    query_low = rotate(
        qkv_lin[:, 0].reshape(row_count, heads_here, HEAD), cosine_table, sine_table, ROT // 2
    ).astype(low_type)
    key_low = rotate(
        qkv_lin[:, 1].reshape(row_count, heads_here, HEAD), cosine_table, sine_table, ROT // 2
    ).astype(low_type)
    value_low = qkv_lin[:, 2].reshape(row_count, heads_here, HEAD).astype(low_type)
    scale_value = HEAD ** (-0.5)
    block_rows = min(row_count, 512)
    block_index = 0
    row_start = block_index * block_rows
    scores = score_block(query_low, key_low, positions, row_start, scale_value)
    row_max = jnp.max(scores, -1, keepdims=True)
    exp_scores = jnp.exp(scores - row_max)
    row_total = jnp.sum(exp_scores, -1, keepdims=True)
    soft_low = (exp_scores / row_total).astype(low_type)
    attended_parts = jnp.einsum(
        "hqk,khe->qhe", soft_low, value_low, preferred_element_type=jnp.float32
    ).astype(low_type)
    lse_parts = [row_max + jnp.log(row_total)]
    attended_flat = attended_parts.reshape(row_count, head_width)
    up_lin = jnp.dot(gathered, up_full, preferred_element_type=jnp.float32) + up_bias
    activated, gelu_back = jax.vjp(gelu_tanh, up_lin)
    activated_low = activated.astype(low_type)
    partial_sum = jnp.dot(attended_flat, out_full, preferred_element_type=jnp.float32) + jnp.dot(
        activated_low, down_full, preferred_element_type=jnp.float32
    )
    summed = lax.psum_scatter(
        partial_sum.astype(jnp.bfloat16), "tensor", scatter_dimension=0, tiled=True
    ).astype(jnp.float32)
    layer_out = (residual + summed + vector_table[5] + vector_table[6]).astype(low_type)
    cot_full = lax.all_gather(cotangent, "tensor", axis=0, tiled=True)
    grad_act = jnp.einsum("rd,fd->rf", cot_full, down_full, preferred_element_type=jnp.float32)
    grad_up_lin = gelu_back(grad_act)[0].astype(low_type)
    grad_down_w = jnp.einsum(
        "rf,rd->fd", activated_low, cot_full, preferred_element_type=jnp.float32
    )
    grad_up_w = jnp.einsum("rd,rf->df", gathered, grad_up_lin, preferred_element_type=jnp.float32)
    up_bias_grad = jnp.sum(grad_up_lin.astype(jnp.float32), 0)
    grad_out_w = jnp.einsum(
        "rn,rd->nd", attended_flat, cot_full, preferred_element_type=jnp.float32
    )
    grad_attended = jnp.einsum(
        "rd,nd->rn", cot_full, out_full, preferred_element_type=jnp.float32
    ).astype(low_type)
    grad_attended = grad_attended.reshape(row_count, heads_here, HEAD)
    block_index = 0
    row_start = block_index * block_rows
    scores = score_block(query_low, key_low, positions, row_start, scale_value)
    soft_full = jnp.exp(scores - lse_parts[block_index])
    soft_low = soft_full.astype(low_type)
    grad_values = jnp.einsum(
        "hqk,qhe->khe", soft_low, grad_attended, preferred_element_type=jnp.float32
    )
    grad_soft = jnp.einsum(
        "qhe,khe->hqk", grad_attended, value_low, preferred_element_type=jnp.float32
    )
    row_delta = jnp.sum(soft_full * grad_soft, -1, keepdims=True)
    grad_scores = (soft_full * (grad_soft - row_delta)).astype(low_type)
    query_parts = (
        jnp.einsum("hqk,khe->qhe", grad_scores, key_low, preferred_element_type=jnp.float32)
        * scale_value
    )
    grad_keys = (
        jnp.einsum("hqk,qhe->khe", grad_scores, query_low, preferred_element_type=jnp.float32)
        * scale_value
    )
    grad_query = unrotate(query_parts, cosine_table, sine_table, ROT // 2)
    grad_keys = unrotate(grad_keys, cosine_table, sine_table, ROT // 2)
    grad_qkv_lin = (
        jnp.stack([grad_query, grad_keys, grad_values], 1)
        .reshape(row_count, 3, head_width)
        .astype(low_type)
    )
    grad_qkv_w = jnp.einsum(
        "rd,rcn->dcn", gathered, grad_qkv_lin, preferred_element_type=jnp.float32
    )
    qkv_bias_grad = jnp.sum(grad_qkv_lin.astype(jnp.float32), 0)
    reduced_qkv, reduced_out, reduced_up, reduced_down = (
        lax.psum_scatter(
            grad_qkv_w.astype(jnp.bfloat16), "dp", scatter_dimension=0, tiled=True
        ).astype(jnp.float32),
        lax.psum_scatter(
            grad_out_w.astype(jnp.bfloat16), "dp", scatter_dimension=1, tiled=True
        ).astype(jnp.float32),
        lax.psum_scatter(
            grad_up_w.astype(jnp.bfloat16), "dp", scatter_dimension=0, tiled=True
        ).astype(jnp.float32),
        lax.psum_scatter(
            grad_down_w.astype(jnp.bfloat16), "dp", scatter_dimension=1, tiled=True
        ).astype(jnp.float32),
    )
    grad_hidden_part = jnp.einsum(
        "rcn,dcn->rd", grad_qkv_lin, qkv_full, preferred_element_type=jnp.float32
    )
    grad_hidden_part = grad_hidden_part + jnp.einsum(
        "rf,df->rd", grad_up_lin, up_full, preferred_element_type=jnp.float32
    )
    grad_hidden = lax.psum_scatter(
        grad_hidden_part.astype(jnp.bfloat16), "tensor", scatter_dimension=0, tiled=True
    ).astype(jnp.float32)
    cot_local = cotangent.astype(jnp.float32)
    grad_hat = grad_hidden * norm_gain
    input_grad = cot_local + scale_inv * (
        grad_hat
        - jnp.mean(grad_hat, -1, keepdims=True)
        - normed * jnp.mean(grad_hat * normed, -1, keepdims=True)
    )
    gain_grad = jnp.sum(grad_hidden * normed, 0)
    shift_grad = jnp.sum(grad_hidden, 0)
    out_bias_grad = jnp.sum(cot_local, 0)
    qkv_rows = lax.dynamic_update_slice(
        jnp.zeros((3, feature_width), jnp.float32), qkv_bias_grad, (0, tensor_rank * head_width)
    )
    up_row = lax.dynamic_update_slice(
        jnp.zeros(((vector_table.shape[0] - 7) * feature_width,), jnp.float32),
        up_bias_grad,
        (tensor_rank * hidden_width,),
    )
    vector_part = jnp.concatenate(
        [
            gain_grad[None],
            shift_grad[None],
            qkv_rows,
            out_bias_grad[None],
            out_bias_grad[None],
            up_row.reshape(-1, feature_width),
        ],
        0,
    )
    vector_grad = lax.psum_scatter(vector_part, ("dp", "tensor"), scatter_dimension=1, tiled=True)
    first_new = first_decay * vector_first + (1.0 - first_decay) * vector_grad
    second_new = second_decay * vector_second + (1.0 - second_decay) * vector_grad * vector_grad
    first_hat = first_new / (1.0 - first_decay**STEP)
    second_hat = second_new / (1.0 - second_decay**STEP)
    vectors_new = vectors - adam_rate * first_hat / (jnp.sqrt(second_hat) + adam_epsilon)
    qkv_moment_new = muon_decay * qkv_moment + reduced_qkv
    out_moment_new = muon_decay * out_moment + reduced_out
    up_moment_new = muon_decay * up_moment + reduced_up
    down_moment_new = muon_decay * down_moment + reduced_down
    nesterov_qkv = (reduced_qkv + muon_decay * qkv_moment_new).reshape(qkv_moment.shape[0], -1)
    nesterov_out = reduced_out + muon_decay * out_moment_new
    nesterov_up = reduced_up + muon_decay * up_moment_new
    nesterov_down = reduced_down + muon_decay * down_moment_new
    pieces = jnp.concatenate(
        [
            column_blocks(nesterov_qkv),
            nesterov_out.reshape(-1, BR, nesterov_out.shape[1]),
            column_blocks(nesterov_up),
            nesterov_down.reshape(-1, BR, nesterov_down.shape[1]),
        ],
        0,
    )
    piece_count = pieces.shape[0]
    rank_count = lax.axis_size("dp")
    slot_count = (piece_count + rank_count - 1) // rank_count
    padded = jnp.concatenate(
        [
            pieces,
            jnp.zeros((slot_count * rank_count - piece_count,) + pieces.shape[1:], jnp.float32),
        ],
        0,
    )
    outgoing = padded.reshape(slot_count, rank_count, BR, -1).transpose(1, 0, 2, 3)
    orthogonal = owner_work(
        lax.all_to_all(
            outgoing.astype(jnp.bfloat16), "dp", split_axis=0, concat_axis=0, tiled=True
        ).astype(outgoing.dtype)
    )
    returned = lax.all_to_all(
        as_sent(orthogonal), "dp", split_axis=0, concat_axis=0, tiled=True
    ).astype(orthogonal.dtype)
    updates = returned.transpose(1, 0, 2, 3).reshape(slot_count * rank_count, BR, -1)[:piece_count]
    count_qkv = nesterov_qkv.shape[1] // BR
    count_out = nesterov_out.shape[0] // BR
    count_up = nesterov_up.shape[1] // BR
    update_qkv = column_restore(updates[:count_qkv], nesterov_qkv.shape).reshape(qkv_weight.shape)
    update_out = updates[count_qkv : count_qkv + count_out].reshape(out_weight.shape)
    update_up = column_restore(
        updates[count_qkv + count_out : count_qkv + count_out + count_up], up_weight.shape
    )
    update_down = updates[count_qkv + count_out + count_up :].reshape(down_weight.shape)
    qkv_new = qkv_weight * (1.0 - decay_factor * rate_qkv) - rate_qkv * update_qkv
    out_new = out_weight * (1.0 - decay_factor * rate_out) - rate_out * update_out
    up_new = up_weight * (1.0 - decay_factor * rate_up) - rate_up * update_up
    down_new = down_weight * (1.0 - decay_factor * rate_down) - rate_down * update_down
    return (
        layer_out,
        input_grad,
        qkv_new,
        out_new,
        up_new,
        down_new,
        qkv_moment_new,
        out_moment_new,
        up_moment_new,
        down_moment_new,
        first_new,
        second_new,
        vectors_new,
    )


def solution(mesh):
    in_specs = (
        P(("dp", "tensor"), None),
        P(("dp", "tensor"), None),
        P("dp"),
        P("dp", None, "tensor"),
        P("tensor", "dp"),
        P("dp", "tensor"),
        P("tensor", "dp"),
        P("dp", None, "tensor"),
        P("tensor", "dp"),
        P("dp", "tensor"),
        P("tensor", "dp"),
        P(None, ("dp", "tensor")),
        P(None, ("dp", "tensor")),
        P(None, ("dp", "tensor")),
    )
    out_specs = (
        P(("dp", "tensor"), None),
        P(("dp", "tensor"), None),
        P("dp", None, "tensor"),
        P("tensor", "dp"),
        P("dp", "tensor"),
        P("tensor", "dp"),
        P("dp", None, "tensor"),
        P("tensor", "dp"),
        P("dp", "tensor"),
        P("tensor", "dp"),
        P(None, ("dp", "tensor")),
        P(None, ("dp", "tensor")),
        P(None, ("dp", "tensor")),
    )
    return jax.shard_map(local, mesh=mesh, in_specs=in_specs, out_specs=out_specs, check_vma=False)
```

profile of v0, /device:TPU:0, one launch (start us, length us, event | category | flops | bytes accessed | tf_op | source)
XLA Modules:
  0.0 1379.8 jit_solution(8702286842607767631)
XLA Ops:
  10.4 64.7 %all_gather.21 = f32[11,2048]{0,1:T(8,128)S(1)} all-gather(f32[11,16]{0,1:T(8,128)S(1)} %copy.106), channel_id=1, replica_groups=mesh['dp'=32,'tensor'=4] {'dp','tensor'}, dimensions={1}, use_global_device_ids=true | all-gather | bytes 90816 | tf_op jit(solution)/shard_map/all_gather | solution.py:150
  77.7 2.3 slice_reduce_fusion.1
  86.7 3.4 all-gather.11.cloned.1.call-done
  90.2 3.5 convolution_convert_fusion.4
  93.7 29.0 %all-gather.7.cloned.1.call-done = bf16[512,2048]{1,0:T(8,128)(2,1)} async-done(((bf16[128,2048]{1,0:T(8,128)(2,1)}), bf16[512,2048]{1,0:T(8,128)(2,1)}) %all-gather.7.cloned.1.call-update) | async-done | bytes 2097168 | tf_op jit(solution)/shard_map/all_gather | solution.py:168
  122.7 51.7 %all-gather.9.cloned.1.call-done = bf16[2048,3,512]{2,0,1:T(8,128)(2,1)} async-done(((bf16[64,3,512]{2,0,1:T(8,128)(2,1)}), bf16[2048,3,512]{2,0,1:T(8,128)(2,1)}) %all-gather.9.cloned.1.call-update) | async-done | bytes 6291472 | tf_op jit(solution)/shard_map/all_gather | solution.py:145
  174.4 6.3 fusion.21
  184.5 2.0 copy-done
  188.9 2.6 convolution_convert_fusion.3
  191.8 5.5 multiply_reduce_fusion
  197.8 2.5 multiply_convert_fusion
  205.2 6.5 fusion.30
  212.9 7.3 convolution_convert_fusion.2
  221.4 7.5 all-gather.13.cloned.1.call-done
  228.9 7.6 fusion.72
  236.5 2.0 copy-done.45
  238.5 7.3 convolution_convert_fusion
  245.8 38.2 %all-gather.15.cloned.1.call-done = bf16[2048,2048]{0,1:T(8,128)(2,1)} async-done(((bf16[2048,64]{0,1:T(8,128)(2,1)}), bf16[2048,2048]{0,1:T(8,128)(2,1)}) %all-gather.15.cloned.1.call-update) | async-done | bytes 8388624 | tf_op jit(solution)/shard_map/all_gather | solution.py:148
  284.0 11.1 convert_reduce_fusion
  296.5 6.8 convolution_convert_fusion.1
  304.8 7.7 fusion.73
  312.5 7.7 fusion.11
  320.2 45.8 %reduce-scatter.16.cloned.1.call-done = bf16[512,64]{0,1:T(8,128)(2,1)} async-done(((bf16[512,2048]{0,1:T(8,128)(2,1)}), bf16[512,64]{0,1:T(8,128)(2,1)}) %reduce-scatter.16.cloned.1.call-update) | async-done | bytes 65552 | tf_op jit(solution)/shard_map/reduce_scatter | solution.py:257
  367.5 87.8 %reduce-scatter.14.cloned.1.call-done = bf16[64,3,512]{2,0,1:T(8,128)(2,1)} async-done(((bf16[2048,3,512]{2,0,1:T(8,128)(2,1)}), bf16[64,3,512]{2,0,1:T(8,128)(2,1)}) %reduce-scatter.14.cloned.1.call-update) | async-done | bytes 196624 | tf_op jit(solution)/shard_map/reduce_scatter | solution.py:254
  455.3 1.8 fusion.60
  458.8 92.7 %reduce-scatter.20.cloned.1.call-done = bf16[2048,64]{0,1:T(8,128)(2,1)} async-done(((bf16[2048,2048]{0,1:T(8,128)(2,1)}), bf16[2048,64]{0,1:T(8,128)(2,1)}) %reduce-scatter.20.cloned.1.call-update) | async-done | bytes 262160 | tf_op jit(solution)/shard_map/reduce_scatter | solution.py:263
  551.5 1.8 fusion.57
  553.4 93.7 %reduce-scatter.18.cloned.1.call-done = bf16[64,2048]{1,0:T(8,128)(2,1)} async-done(((bf16[2048,2048]{1,0:T(8,128)(2,1)}), bf16[64,2048]{1,0:T(8,128)(2,1)}) %reduce-scatter.18.cloned.1.call-update) | async-done | bytes 262160 | tf_op jit(solution)/shard_map/reduce_scatter | solution.py:260
  647.1 1.8 fusion.56
  651.1 5.2 all-to-all-start
  656.4 12.1 fusion.67
  668.8 5.6 add_convert_fusion
  674.4 4.5 reduce-scatter.12.cloned.1.call-done
  682.3 3.6 fusion.42
  686.3 2.5 convert_divide_fusion
  688.8 3.7 copy.124
  692.6 3.6 convolution_add_fusion.4
  696.1 1.9 fusion.74
  698.4 2.1 convolution_add_fusion.3
  700.5 1.9 fusion.75
  702.8 2.1 convolution_add_fusion.2
  704.8 2.1 fusion.76
  707.3 2.1 convolution_add_fusion.1
  709.4 1.9 fusion.77
  711.7 2.1 fusion.14
  715.1 7.3 all-to-all-start.1
  722.5 2.9 convert_reduce_fusion.4
  727.0 639.1 %reduce-scatter.22.cloned.1.call-done = f32[16,11]{1,0:T(8,128)} async-done(((f32[2048,11]{1,0:T(8,128)}), f32[16,11]{1,0:T(8,128)}) %reduce-scatter.22.cloned.1.call-update) | async-done | bytes 720
  (211 shorter events, 49.4 us)
Async XLA Ops:
  7.2 73.5 %copy-start.1 = (bf16[128,2048]{1,0:T(8,128)(2,1)S(1)}, bf16[128,2048]{1,0:T(8,128)(2,1)}, u32[]{:S(2)}) copy-start(bf16[128,2048]{1,0:T(8,128)(2,1)} %param.14) | copy-start | bytes 1572868
  7.2 79.5 %all-gather.17.cloned.1.call-start = ((), (), s32[]{:S(2)}) async-start(), calls=%async_computation.15 | async-start | bytes 2621440 | tf_op jit(solution)/shard_map/all_gather | solution.py:206
  7.9 74.0 %copy-start.13 = (f32[64,3,512]{2,0,1:T(8,128)S(1)}, f32[64,3,512]{2,0,1:T(8,128)}, u32[]{:S(2)}) copy-start(f32[64,3,512]{2,0,1:T(8,128)} %param.17) | copy-start | bytes 1179652
  7.9 82.2 %all-gather.11.cloned.1.call-start = ((), (), s32[]{:S(2)}) async-start(), calls=%async_computation.11 | async-start | bytes 2162688 | tf_op jit(solution)/shard_map/all_gather | solution.py:146
  9.6 113.1 %all-gather.7.cloned.1.call-start = ((), (), s32[]{:S(2)}) async-start(), calls=%async_computation.9 | async-start | bytes 2621440 | tf_op jit(solution)/shard_map/all_gather | solution.py:168
  10.4 72.3 %copy-start.6 = (f32[64,2048]{1,0:T(8,128)S(1)}, f32[64,2048]{1,0:T(8,128)}, u32[]{:S(2)}) copy-start(f32[64,2048]{1,0:T(8,128)} %param.19) | copy-start | bytes 1572868
  76.3 7.2 copy-start.4
  76.3 3.7 copy-start.35
  80.1 4.9 copy-start.37
  81.9 92.5 %all-gather.9.cloned.1.call-start = ((), (), s32[]{:S(2)}) async-start(), calls=%async_computation.10 | async-start | bytes 6488064 | tf_op jit(solution)/shard_map/all_gather | solution.py:145
  82.7 146.2 %all-gather.13.cloned.1.call-start = ((), (), s32[]{:S(2)}) async-start(), calls=%async_computation.12 | async-start | bytes 8650752 | tf_op jit(solution)/shard_map/all_gather | solution.py:147
  83.5 200.5 %all-gather.15.cloned.1.call-start = ((), (), s32[]{:S(2)}) async-start(), calls=%async_computation.13 | async-start | bytes 8650752 | tf_op jit(solution)/shard_map/all_gather | solution.py:148
  84.3 281.7 %reduce-scatter.16.cloned.1.call-start = ((), (), s32[]{:S(2)}) async-start(), calls=%async_computation.18 | async-start | bytes 2162688 | tf_op jit(solution)/shard_map/reduce_scatter | solution.py:257
  183.2 3.3 copy-start
  191.5 263.8 %reduce-scatter.14.cloned.1.call-start = ((), (), s32[]{:S(2)}) async-start(), calls=%async_computation.17 | async-start | bytes 6488064 | tf_op jit(solution)/shard_map/reduce_scatter | solution.py:254
  191.8 5.5 slice-start
  191.8 6.0 slice-start.1
  205.1 7.7 copy-start.9
  212.9 7.3 copy-start.11
  220.2 331.3 %reduce-scatter.20.cloned.1.call-start = ((), (), s32[]{:S(2)}) async-start(), calls=%async_computation.20 | async-start | bytes 8650752 | tf_op jit(solution)/shard_map/reduce_scatter | solution.py:263
  221.4 17.1 %copy-start.43 = (bf16[512,2048]{1,0:T(8,128)(2,1)S(1)}, bf16[512,2048]{1,0:T(8,128)(2,1)}, u32[]{:S(2)}) copy-start(bf16[512,2048]{1,0:T(8,128)(2,1)} %all-gather.17.cloned.1.call-done) | copy-start | bytes 6291460
  245.7 401.3 %reduce-scatter.18.cloned.1.call-start = ((), (), s32[]{:S(2)}) async-start(), calls=%async_computation.19 | async-start | bytes 8650752 | tf_op jit(solution)/shard_map/reduce_scatter | solution.py:260
  284.0 12.4 copy-start.44
  303.3 375.6 %reduce-scatter.12.cloned.1.call-start = ((), (), s32[]{:S(2)}) async-start(), calls=%async_computation.16 | async-start | bytes 2621440 | tf_op jit(solution)/shard_map/reduce_scatter | solution.py:273
  312.5 53.5 %copy-start.31 = (f32[512,64]{0,1:T(8,128)S(1)}, f32[512,64]{0,1:T(8,128)}, u32[]{:S(2)}) copy-start(f32[512,64]{0,1:T(8,128)} %param.22) | copy-start | bytes 393220
  312.5 142.8 %copy-start.23 = (f32[64,3,512]{2,0,1:T(8,128)S(1)}, f32[64,3,512]{2,0,1:T(8,128)}, u32[]{:S(2)}) copy-start(f32[64,3,512]{2,0,1:T(8,128)} %param.21) | copy-start | bytes 1179652
  320.2 231.3 %copy-start.15 = (f32[2048,64]{0,1:T(8,128)S(1)}, f32[2048,64]{0,1:T(8,128)}, u32[]{:S(2)}) copy-start(f32[2048,64]{0,1:T(8,128)} %param.24) | copy-start | bytes 1572868
  320.2 326.8 %copy-start.16 = (f32[64,2048]{1,0:T(8,128)S(1)}, f32[64,2048]{1,0:T(8,128)}, u32[]{:S(2)}) copy-start(f32[64,2048]{1,0:T(8,128)} %param.23) | copy-start | bytes 1572868
  651.1 29.4 %all-to-all-start = ((bf16[32,1,256,64]{2,3,1,0:T(8,128)(2,1)}), bf16[32,1,256,64]{2,3,1,0:T(8,128)(2,1)S(1)}, u32[]{:S(2)}, u32[]{:S(2)}) async-start(bf16[32,1,256,64]{2,3,1,0:T(8,128)(2,1)} %broadcast_dynamic-update-slice_fusion), calls=%async_computation.6 | async-start | bytes 2097152 | tf_op jit(solution)/shard_map/all_to_all | solution.py:340
  656.3 12.4 copy-start.18
  656.4 66.1 %reduce-scatter.10.cloned.1.call-start = ((), (), s32[]{:S(2)}) async-start(), calls=%async_computation.14 | async-start | bytes 2621440 | tf_op jit(solution)/shard_map/reduce_scatter | solution.py:202
  668.8 10.1 copy-start.30
  668.8 10.1 copy-start.36
  668.8 10.1 copy-start.41
  688.8 3.7 copy-start.2
  711.3 11.2 copy-start.3
  711.3 11.2 copy-start.8
  711.3 11.2 copy-start.32
  711.3 11.2 copy-start.33
  715.1 651.8 %copy-start.34 = (f32[11,16]{1,0:T(8,128)S(1)}, f32[11,16]{1,0:T(8,128)}, u32[]{:S(2)}) copy-start(f32[11,16]{1,0:T(8,128)} %param.25) | copy-start | bytes 2116
  715.1 651.8 %copy-start.38 = (f32[11,16]{1,0:T(8,128)S(1)}, f32[11,16]{1,0:T(8,128)}, u32[]{:S(2)}) copy-start(f32[11,16]{1,0:T(8,128)} %param.27) | copy-start | bytes 2116
  715.1 651.8 %copy-start.39 = (f32[11,16]{1,0:T(8,128)S(1)}, f32[11,16]{1,0:T(8,128)}, u32[]{:S(2)}) copy-start(f32[11,16]{1,0:T(8,128)} %param.26) | copy-start | bytes 2116
  715.1 652.4 %all-to-all-start.1 = ((bf16[32,1,256,64]{2,3,1,0:T(8,128)(2,1)}), bf16[32,1,256,64]{2,3,1,0:T(8,128)(2,1)S(1)}, u32[]{:S(2)}, u32[]{:S(2)}) async-start(bf16[32,1,256,64]{2,3,1,0:T(8,128)(2,1)} %bitcast.29), calls=%async_computation.7 | async-start | bytes 2097152 | tf_op jit(solution)/shard_map/all_to_all | solution.py:344
  722.4 643.7 %reduce-scatter.22.cloned.1.call-start = ((), (), s32[]{:S(2)}) async-start(), calls=%async_computation.21 | async-start | bytes 1056768
  727.0 642.1 %copy-start.14 = (f32[64,3,512]{2,0,1:T(8,128)S(1)}, f32[64,3,512]{2,0,1:T(8,128)}, u32[]{:S(2)}) copy-start(f32[64,3,512]{2,0,1:T(8,128)} %param.17) | copy-start | bytes 1179652
  1367.9 3.4 copy-start.7
  1369.1 3.1 copy-start.22
  1369.1 3.3 copy-start.21
  (16 other events, 21.0 us)
Sparse Core Ops, SparseCore 0:
  9.7 33.6 all-gather.16
  46.2 43.9 all-gather.10
  92.4 30.2 all-gather.6
  125.5 48.8 all-gather.8
  177.1 51.7 all-gather.12
  231.6 52.3 all-gather.14
  287.6 78.3 reduce-scatter.15
  369.7 85.5 reduce-scatter.13
  459.5 91.9 reduce-scatter.19
  555.0 91.9 reduce-scatter.17
  649.6 29.2 reduce-scatter.11
  681.2 29.4 reduce-scatter.9
  727.1 638.9 reduce-scatter.21
where the time goes:
time: 1380 us
  waiting for transfers between devices  1090 us (79%)
  matrix products  128 us (9%)
  blocking collectives  64.7 us (5%)
  other arithmetic  34 us (2%)
  local copies, waits for them, and re-layouts  29.3 us (2%)
  between operations  15.7 us (1%)
  starting transfers between devices  14 us (1%)
    unnamed x14, waiting for transfers between devices  640 us
    reduce_scatter x1, waiting for transfers between devices, local(): lax.psum_scatter(grad_up_w.astype(jnp.bfloat16), 'dp', scatter_dimension=...  93.7 us
    reduce_scatter x1, waiting for transfers between devices, local(): lax.psum_scatter(grad_down_w.astype(jnp.bfloat16), 'dp', scatter_dimensio...  92.7 us
    reduce_scatter x1, waiting for transfers between devices, local(): lax.psum_scatter(grad_qkv_w.astype(jnp.bfloat16), 'dp', scatter_dimension...  87.8 us
    all_gather x1, blocking collectives, local(): vector_table = lax.all_gather(vectors, ('dp', 'tensor'), axis=1, tiled=True)  64.7 us
    all_gather x1, waiting for transfers between devices, local(): lax.all_gather(qkv_weight.astype(low_type), 'dp', axis=0, tiled=True)  51.7 us
    reduce_scatter x1, waiting for transfers between devices, local(): lax.psum_scatter(grad_out_w.astype(jnp.bfloat16), 'dp', scatter_dimension...  45.8 us
    all_gather x1, waiting for transfers between devices, local(): lax.all_gather(down_weight.astype(low_type), 'dp', axis=1, tiled=True)  38.2 us
  transfers between devices with their start and end apart: 15, of which 11 were waited for; matrix products, arithmetic and copies ran while one was open for 13% of the time, Pallas kernels for 0%

commit v1 on v0

v1 whole, which is shorter than its diff:
```python
import jax
import jax.numpy as jnp
from jax import lax
from jax.sharding import Mesh
from jax.sharding import PartitionSpec as P

HEAD = 64
ROT = 32
BR = 256
SWEEPS = 5
STEP = 10

highest = lax.Precision.HIGHEST
norm_epsilon = 1e-05
ortho_epsilon = 1e-07
masked_score = -1e30
rotary_base = 10000.0
muon_decay = 0.95
coef_linear = 3.4445
coef_square = -4.775
coef_cubic = 2.0315
decay_factor = 0.01
rate_qkv = 1.0
rate_out = 4.0
rate_up = 0.8
rate_down = 0.4
adam_rate = 0.2
first_decay = 0.9
second_decay = 0.95
adam_epsilon = 1e-08

f32 = jnp.float32
bf16 = jnp.bfloat16
PLANE = ("x", "y")
GROUP = ("core", "tensor")
DP = ("x", "y", "core")
ALL = ("x", "y", "core", "tensor")


def rotary_tables(positions, half_rot):
    freq_index = jnp.arange(half_rot).astype(f32)
    inverse_freq = rotary_base ** (-2.0 * freq_index / (2 * half_rot))
    angles = positions.astype(f32)[:, None] * inverse_freq[None, :]
    return (jnp.cos(angles)[:, None, :], jnp.sin(angles)[:, None, :])


def rotate(vectors_in, cosine_table, sine_table, half_rot):
    first_half = vectors_in[..., :half_rot]
    second = vectors_in[..., half_rot : 2 * half_rot]
    remainder = vectors_in[..., 2 * half_rot :]
    return jnp.concatenate(
        [
            first_half * cosine_table - second * sine_table,
            second * cosine_table + first_half * sine_table,
            remainder,
        ],
        -1,
    )


def unrotate(grads_in, cosine_table, sine_table, half_rot):
    first_half = grads_in[..., :half_rot]
    second = grads_in[..., half_rot : 2 * half_rot]
    remainder = grads_in[..., 2 * half_rot :]
    return jnp.concatenate(
        [
            first_half * cosine_table + second * sine_table,
            second * cosine_table - first_half * sine_table,
            remainder,
        ],
        -1,
    )


def gelu_tanh(values):
    return jax.nn.gelu(values, approximate=True)


def fold_in(qkv, up):
    rows = qkv.shape[0]
    halves = qkv.shape[2] // 2
    qkv_part = qkv.reshape(rows, 3, 2, halves).transpose(2, 0, 1, 3).reshape(2, rows, 3 * halves)
    up_part = up.reshape(rows, 2, -1).transpose(1, 0, 2)
    return jnp.concatenate([qkv_part, up_part], -1)


def fold_out(out, down):
    width = out.shape[1]
    out_part = out.reshape(2, -1, width).transpose(0, 2, 1)
    down_part = down.reshape(2, -1, width).transpose(0, 2, 1)
    return jnp.concatenate([out_part, down_part], -1)


def unfold_in(both, qkv_shape, up_shape):
    rows = both.shape[1]
    halves = qkv_shape[2] // 2
    qkv = both[:, :, : 3 * halves].reshape(2, rows, 3, halves).transpose(1, 2, 0, 3)
    up = both[:, :, 3 * halves :].transpose(1, 0, 2)
    return qkv.reshape(qkv_shape), up.reshape(up_shape)


def unfold_out(both, out_shape, down_shape):
    out_rows = out_shape[0] // 2
    out = both[:, :, :out_rows].transpose(0, 2, 1).reshape(out_shape)
    down = both[:, :, out_rows:].transpose(0, 2, 1).reshape(down_shape)
    return out, down


def orthogonalize(tall):
    norm = jnp.sqrt(jnp.sum(tall * tall))
    current = tall / (norm + ortho_epsilon)
    for sweep_index in range(SWEEPS):
        gram = jnp.einsum("ki,kj->ij", current, current, precision=highest)
        polynomial = coef_square * gram + coef_cubic * jnp.dot(gram, gram, precision=highest)
        current = coef_linear * current + jnp.dot(current, polynomial, precision=highest)
    return current


def gather_weights(low):
    mine = lax.all_to_all(low, "core", split_axis=0, concat_axis=0, tiled=True)
    mine = mine.reshape(2 * low.shape[1], low.shape[2])
    return lax.all_gather(mine, PLANE, axis=0, tiled=True)


def reduce_weights(grad):
    mine = lax.psum_scatter(grad, PLANE, scatter_dimension=0, tiled=True)
    mine = mine.reshape(2, mine.shape[0] // 2, mine.shape[1])
    return lax.all_to_all(mine, "core", split_axis=0, concat_axis=0, tiled=True)


def local(
    inputs,
    cotangent,
    positions,
    qkv_weight,
    out_weight,
    up_weight,
    down_weight,
    qkv_moment,
    out_moment,
    up_moment,
    down_moment,
    vectors,
    vector_first,
    vector_second,
):
    core = lax.axis_index("core")
    tensor_rank = lax.axis_index("tensor")
    device_rank = lax.axis_index(ALL)
    feature = inputs.shape[1]

    in_full = gather_weights(fold_in(qkv_weight, up_weight).astype(bf16))
    out_full = gather_weights(fold_out(out_weight, down_weight).astype(bf16))
    tokens = lax.all_gather(inputs, GROUP, axis=0, tiled=True)
    cot_full = lax.all_gather(cotangent, GROUP, axis=0, tiled=True)
    position_full = lax.all_gather(positions, "core", axis=0, tiled=True)

    vector_rows, vector_width = vectors.shape
    packed = jnp.pad(vectors.reshape(1, -1), ((0, 0), (0, 256 - vector_rows * vector_width)))
    packed = lax.all_gather(packed, ALL, axis=0, tiled=True)
    vector_table = (
        packed[:, : vector_rows * vector_width]
        .reshape(-1, vector_rows, vector_width)
        .transpose(1, 0, 2)
        .reshape(vector_rows, feature)
    )

    head_width = qkv_weight.shape[2] // 2
    hidden_width = up_weight.shape[1] // 2
    part = tensor_rank * 2 + core
    qkv_bias = lax.dynamic_slice_in_dim(vector_table[2:5], part * head_width, head_width, 1)
    up_bias = lax.dynamic_slice_in_dim(
        vector_table[7:].reshape(-1), part * hidden_width, hidden_width, 0
    )
    norm_gain = vector_table[0]
    norm_shift = vector_table[1]

    def standardize(rows):
        residual = rows.astype(f32)
        center = residual - jnp.mean(residual, -1, keepdims=True)
        variance = jnp.mean(center * center, -1, keepdims=True)
        scale_inv = lax.rsqrt(variance + norm_epsilon)
        return residual, center * scale_inv, scale_inv

    hidden = (standardize(tokens)[1] * norm_gain + norm_shift).astype(bf16)
    row_count = hidden.shape[0]
    heads = head_width // HEAD
    groups = 2
    group_rows = row_count // groups

    in_lin = jnp.dot(hidden, in_full, preferred_element_type=f32)
    qkv_lin = in_lin[:, : 3 * head_width].reshape(row_count, 3, head_width) + qkv_bias[None]
    up_lin = in_lin[:, 3 * head_width :] + up_bias
    cosine_table, sine_table = rotary_tables(position_full, ROT // 2)

    def headed(part_in):
        return part_in.reshape(row_count, heads, HEAD)

    def grouped(part_in):
        return part_in.reshape(groups, group_rows, heads, HEAD)

    query_low = grouped(
        rotate(headed(qkv_lin[:, 0]), cosine_table, sine_table, ROT // 2).astype(bf16)
    )
    key_low = grouped(
        rotate(headed(qkv_lin[:, 1]), cosine_table, sine_table, ROT // 2).astype(bf16)
    )
    value_low = grouped(headed(qkv_lin[:, 2]).astype(bf16))
    scale_value = HEAD ** (-0.5)
    ids = jnp.arange(group_rows)
    position_group = position_full.reshape(groups, group_rows)
    visible = (ids[None, None, :] <= ids[None, :, None]) & (
        ids[None, :, None] - ids[None, None, :] <= position_group[:, :, None]
    )
    scores = (
        jnp.einsum("gqhe,gkhe->ghqk", query_low, key_low, preferred_element_type=f32)
        * scale_value
    )
    scores = jnp.where(visible[:, None], scores, masked_score)
    row_max = jnp.max(scores, -1, keepdims=True)
    exp_scores = jnp.exp(scores - row_max)
    soft = exp_scores / jnp.sum(exp_scores, -1, keepdims=True)
    soft_low = soft.astype(bf16)
    attended = jnp.einsum(
        "ghqk,gkhe->gqhe", soft_low, value_low, preferred_element_type=f32
    ).astype(bf16)
    activated, gelu_back = jax.vjp(gelu_tanh, up_lin)
    middle = jnp.concatenate(
        [attended.reshape(row_count, head_width), activated.astype(bf16)], -1
    )
    partial_sum = lax.dot_general(
        middle, out_full, (((1,), (1,)), ((), ())), preferred_element_type=f32
    )
    summed = lax.psum_scatter(
        partial_sum.astype(bf16), GROUP, scatter_dimension=0, tiled=True
    ).astype(f32)

    grad_middle = jnp.dot(cot_full, out_full, preferred_element_type=f32)
    grad_up_lin = gelu_back(grad_middle[:, head_width:])[0].astype(bf16)
    grad_attended = grouped(headed(grad_middle[:, :head_width].astype(bf16)))
    grad_out_full = lax.dot_general(
        cot_full, middle, (((0,), (0,)), ((), ())), preferred_element_type=f32
    )

    grad_values = jnp.einsum(
        "ghqk,gqhe->gkhe", soft_low, grad_attended, preferred_element_type=f32
    )
    grad_soft = jnp.einsum(
        "gqhe,gkhe->ghqk", grad_attended, value_low, preferred_element_type=f32
    )
    row_delta = jnp.sum(soft * grad_soft, -1, keepdims=True)
    grad_scores = (soft * (grad_soft - row_delta)).astype(bf16)
    grad_query = (
        jnp.einsum("ghqk,gkhe->gqhe", grad_scores, key_low, preferred_element_type=f32)
        * scale_value
    )
    grad_keys = (
        jnp.einsum("ghqk,gqhe->gkhe", grad_scores, query_low, preferred_element_type=f32)
        * scale_value
    )

    def flat(part_in):
        return part_in.reshape(row_count, heads, HEAD)

    grad_in = jnp.concatenate(
        [
            unrotate(flat(grad_query), cosine_table, sine_table, ROT // 2)
            .reshape(row_count, head_width)
            .astype(bf16),
            unrotate(flat(grad_keys), cosine_table, sine_table, ROT // 2)
            .reshape(row_count, head_width)
            .astype(bf16),
            grad_values.reshape(row_count, head_width).astype(bf16),
            grad_up_lin,
        ],
        -1,
    )
    grad_in_full = lax.dot_general(
        hidden, grad_in, (((0,), (0,)), ((), ())), preferred_element_type=f32
    )
    bias_grad = jnp.sum(grad_in.astype(f32), 0)
    reduced_in = reduce_weights(grad_in_full.astype(bf16)).astype(f32)
    reduced_out = reduce_weights(grad_out_full.astype(bf16)).astype(f32)

    grad_hidden_part = lax.dot_general(
        grad_in, in_full, (((1,), (1,)), ((), ())), preferred_element_type=f32
    )
    grad_hidden = lax.psum_scatter(
        grad_hidden_part.astype(bf16), GROUP, scatter_dimension=0, tiled=True
    ).astype(f32)

    residual, normed, scale_inv = standardize(inputs)
    layer_out = (residual + summed + vector_table[5] + vector_table[6]).astype(bf16)
    cot_local = cotangent.astype(f32)
    grad_hat = grad_hidden * norm_gain
    input_grad = cot_local + scale_inv * (
        grad_hat
        - jnp.mean(grad_hat, -1, keepdims=True)
        - normed * jnp.mean(grad_hat * normed, -1, keepdims=True)
    )
    gain_grad = jnp.sum(grad_hidden * normed, 0)
    shift_grad = jnp.sum(grad_hidden, 0)
    out_bias_grad = jnp.sum(cot_local, 0)
    qkv_rows = lax.dynamic_update_slice(
        jnp.zeros((3, feature), f32),
        bias_grad[: 3 * head_width].reshape(3, head_width),
        (0, part * head_width),
    )
    up_row = lax.dynamic_update_slice(
        jnp.zeros(((vector_rows - 7) * feature,), f32),
        bias_grad[3 * head_width :],
        (part * hidden_width,),
    )
    vector_part = jnp.concatenate(
        [
            gain_grad[None],
            shift_grad[None],
            qkv_rows,
            out_bias_grad[None],
            out_bias_grad[None],
            up_row.reshape(-1, feature),
        ],
        0,
    )
    vector_sum = lax.psum(vector_part, ALL)
    vector_grad = lax.dynamic_slice_in_dim(vector_sum, device_rank * vector_width, vector_width, 1)
    first_new = first_decay * vector_first + (1.0 - first_decay) * vector_grad
    second_new = second_decay * vector_second + (1.0 - second_decay) * vector_grad * vector_grad
    first_hat = first_new / (1.0 - first_decay**STEP)
    second_hat = second_new / (1.0 - second_decay**STEP)
    vectors_new = vectors - adam_rate * first_hat / (jnp.sqrt(second_hat) + adam_epsilon)

    moment_in = muon_decay * fold_in(qkv_moment, up_moment) + reduced_in
    moment_out = muon_decay * fold_out(out_moment, down_moment) + reduced_out
    nesterov_in = reduced_in + muon_decay * moment_in
    nesterov_out = reduced_out + muon_decay * moment_out

    def cut(both):
        halves, rows, columns = both.shape
        return both.reshape(halves, rows, columns // BR, BR).transpose(0, 2, 1, 3).reshape(
            -1, rows, BR
        )

    def paste(pieces):
        rows = pieces.shape[1]
        return (
            pieces.reshape(2, -1, rows, BR).transpose(0, 2, 1, 3).reshape(2, rows, -1)
        )

    pieces = jnp.concatenate([cut(nesterov_in), cut(nesterov_out)], 0).astype(bf16)
    piece_count = pieces.shape[0]
    count_in = 2 * nesterov_in.shape[2] // BR
    rank_count = lax.axis_size(DP)
    outgoing = jnp.concatenate(
        [pieces, jnp.zeros((rank_count - piece_count,) + pieces.shape[1:], bf16)], 0
    )
    received = lax.all_to_all(outgoing, DP, split_axis=0, concat_axis=0, tiled=True)
    orthogonal = orthogonalize(received.reshape(-1, BR).astype(f32))
    returned = lax.all_to_all(
        orthogonal.astype(bf16).reshape(received.shape), DP, split_axis=0, concat_axis=0, tiled=True
    ).astype(f32)
    update_qkv, update_up = unfold_in(paste(returned[:count_in]), qkv_weight.shape, up_weight.shape)
    update_out, update_down = unfold_out(
        paste(returned[count_in:piece_count]), out_weight.shape, down_weight.shape
    )
    qkv_moment_new, up_moment_new = unfold_in(moment_in, qkv_weight.shape, up_weight.shape)
    out_moment_new, down_moment_new = unfold_out(moment_out, out_weight.shape, down_weight.shape)
    qkv_new = qkv_weight * (1.0 - decay_factor * rate_qkv) - rate_qkv * update_qkv
    out_new = out_weight * (1.0 - decay_factor * rate_out) - rate_out * update_out
    up_new = up_weight * (1.0 - decay_factor * rate_up) - rate_up * update_up
    down_new = down_weight * (1.0 - decay_factor * rate_down) - rate_down * update_down
    return (
        layer_out,
        input_grad,
        qkv_new,
        out_new,
        up_new,
        down_new,
        qkv_moment_new,
        out_moment_new,
        up_moment_new,
        down_moment_new,
        first_new,
        second_new,
        vectors_new,
    )


def solution(mesh):
    wide = Mesh(mesh.devices.reshape(4, 4, 2, 4), ALL)
    in_specs = (
        P(ALL, None),
        P(ALL, None),
        P(DP),
        P(DP, None, "tensor"),
        P("tensor", DP),
        P(DP, "tensor"),
        P("tensor", DP),
        P(DP, None, "tensor"),
        P("tensor", DP),
        P(DP, "tensor"),
        P("tensor", DP),
        P(None, ALL),
        P(None, ALL),
        P(None, ALL),
    )
    out_specs = (
        P(ALL, None),
        P(ALL, None),
        P(DP, None, "tensor"),
        P("tensor", DP),
        P(DP, "tensor"),
        P("tensor", DP),
        P(DP, None, "tensor"),
        P("tensor", DP),
        P(DP, "tensor"),
        P("tensor", DP),
        P(None, ALL),
        P(None, ALL),
        P(None, ALL),
    )
    return jax.shard_map(local, mesh=wide, in_specs=in_specs, out_specs=out_specs, check_vma=False)
```

time: 1380 us -> 705 us (0.51)
  waiting for transfers between devices: 1090 us -> 382 us
  local copies, waits for them, and re-layouts: 29.3 us -> 46 us
    unnamed x14 -> x9, waiting for transfers between devices: 640 us -> 1.49 us
    reduce_scatter x6 -> x4, waiting for transfers between devices: 324 us -> 133 us  [the longest x2 83.9 us: reduce_weights(): mine = lax.psum_scatter(grad, PLANE, scatter_dimension=0, tiled=True)]
    psum x0 -> x1, waiting for transfers between devices: none -> 141 us  [local(): vector_sum = lax.psum(vector_part, ALL)]
    all_gather x6 -> x4, waiting for transfers between devices: 130 us -> 107 us  [the longest x2 107 us: gather_weights(): return lax.all_gather(mine, PLANE, axis=0, tiled=True)]
    all_to_all x0 -> x4, blocking collectives: none -> 19.8 us  [the longest x2 10.2 us: reduce_weights(): return lax.all_to_all(mine, 'core', split_axis=0, concat_axis=0, tiled=True)]
    dot_general x33 -> x26, matrix products: 128 us -> 116 us  [the longest x5 18.4 us: orthogonalize(): gram = jnp.einsum('ki,kj->ij', current, current, precision=highest)]
    all_gather x1 -> x2, blocking collectives: 64.7 us -> 57.4 us  [the longest x1 55.6 us: local(): packed = lax.all_gather(packed, ALL, axis=0, tiled=True)]
  transfers between devices with their start and end apart: 15 -> 11, of which waited for: 11 -> 7; matrix products, arithmetic and copies ran while one was open for 13% -> 21% of each run, Pallas kernels for 0% -> 0%
where the time goes in v1:
time: 705 us; the launch traced here: 698 us
  waiting for transfers between devices  382 us (54%)
  matrix products  121 us (17%)
  blocking collectives  77.1 us (11%)
  local copies, waits for them, and re-layouts  46 us (7%)
  other arithmetic  42.8 us (6%)
  between operations  16.1 us (2%)
  starting transfers between devices  12.7 us (2%)
    psum x1, waiting for transfers between devices, local(): vector_sum = lax.psum(vector_part, ALL)  141 us
    all_gather x2, waiting for transfers between devices, gather_weights(): return lax.all_gather(mine, PLANE, axis=0, tiled=True)  107 us
    reduce_scatter x2, waiting for transfers between devices, reduce_weights(): mine = lax.psum_scatter(grad, PLANE, scatter_dimension=0, tiled=True)  83.9 us
    all_gather x1, blocking collectives, local(): packed = lax.all_gather(packed, ALL, axis=0, tiled=True)  55.6 us
    reduce_scatter x1, waiting for transfers between devices, local(): lax.psum_scatter(grad_hidden_part.astype(bf16), GROUP, scatter_dimension=...  36.1 us
    dot_general x5, matrix products, orthogonalize(): gram = jnp.einsum('ki,kj->ij', current, current, precision=highest)  18.4 us
    dot_general x1, matrix products, local(): lax.dot_general(hidden, grad_in, (((0,), (0,)), ((), ())), preferred_elem...  15.4 us
  transfers between devices with their start and end apart: 11, of which 7 were waited for; matrix products, arithmetic and copies ran while one was open for 21% of the time, Pallas kernels for 0%

profile of v1, /device:TPU:0, one launch (start us, length us, event | category | flops | bytes accessed | tf_op | source)
XLA Modules:
  0.0 697.8 jit_solution(738655433150149834)
XLA Ops:
  11.3 4.7 all_to_all.30
  17.5 4.8 all_to_all.31
  24.3 55.6 %all-gather = f32[128,1,256]{2,1,0:T(1,128)S(1)} all-gather(f32[1,1,256]{2,1,0:T(1,128)S(1)} %pad_bitcast_fusion), channel_id=1, replica_groups=mesh['x'=4,'y'=4,'core'=2,'tensor'=4] {'x','y','core','tensor'}, dimensions={0}, use_global_device_ids=true | all-gather | bytes 132096 | tf_op jit(solution)/shard_map/all_gather | solution.py:160
  83.4 3.0 convert_reduce_fusion
  88.1 49.7 %all-gather.11.cloned.1.call-done = bf16[2048,1280]{1,0:T(8,128)(2,1)} async-done(((bf16[128,1280]{1,0:T(8,128)(2,1)}), bf16[2048,1280]{1,0:T(8,128)(2,1)}) %all-gather.11.cloned.1.call-update) | async-done | bytes 5242896 | tf_op jit(solution)/shard_map/all_gather | solution.py:122
  137.8 10.6 %convolution_bitcast_fusion = f32[1024,1280]{1,0:T(8,128)} fusion(bf16[1024,2048]{1,0:T(8,128)(2,1)} %all-gather.13.cloned.1.call-done, bf16[2048,1280]{1,0:T(8,128)(2,1)} %all-gather.11.cloned.1.call-done), kind=kOutput, calls=%fused_computation.20 | convolution fusion | flops 5368709120 | bytes 14680064 | tf_op jit(solution)/shard_map/dot_general | solution.py:238
  148.4 57.2 %all-gather.9.cloned.1.call-done = bf16[2048,1792]{1,0:T(8,128)(2,1)} async-done(((bf16[128,1792]{1,0:T(8,128)(2,1)}), bf16[2048,1792]{1,0:T(8,128)(2,1)}) %all-gather.9.cloned.1.call-update) | async-done | bytes 7340048 | tf_op jit(solution)/shard_map/all_gather | solution.py:122
  205.6 12.2 %fusion.77 = f32[1024,1792]{1,0:T(8,128)S(1)} fusion(bf16[2048,1792]{1,0:T(8,128)(2,1)} %all-gather.9.cloned.1.call-done, bf16[1024,2048]{1,0:T(8,128)(2,1)} %all-gather.7.cloned.1.call-done, f32[2048]{0:T(1024)S(1)} %add.189, f32[2048]{0:T(1024)S(1)} %mul.430, f32[1024]{0:T(1024)S(1)} %add_rsqrt_fusion, f32[1024]{0:T(1024)S(1)} %broadcast_multiply_fusion), kind=kOutput, calls=%fused_computation.181 | convolution fusion | flops 7528775680 | bytes 18898944 | tf_op jit(solution)/shard_map/dot_general | solution.py:191
  217.9 2.9 copy-done.3
  221.0 2.3 copy.145
  223.3 2.2 broadcast_add_fusion
  227.4 5.4 fusion.82
  232.9 4.2 fusion.44
  238.5 5.6 fusion.15
  245.4 8.0 %fusion.7 = bf16[2048,1280]{0,1:T(8,128)(2,1)} fusion(bf16[1024,2048]{1,0:T(8,128)(2,1)S(1)} %copy-done.41, bf16[1024,1024]{1,0:T(8,128)(2,1)S(1)} %get-tuple-element.21, bf16[1024,256]{1,0:T(8,128)(2,1)S(1)} %reshape.370), kind=kOutput, calls=%fused_computation.16 | convolution fusion | flops 5376573440 | bytes 12058624 | tf_op jit(solution)/shard_map/dot_general | solution.py:241
  253.4 7.9 %copy.198 = bf16[2048,1280]{1,0:T(8,128)(2,1)} copy(bf16[2048,1280]{0,1:T(8,128)(2,1)} %fusion.7) | data formatting | bytes 10485760
  261.4 2.1 slice.298
  263.4 2.0 reshape.374
  266.8 5.8 fusion.41
  275.6 5.1 multiply_reduce_fusion
  280.8 4.9 multiply_convert_fusion
  291.2 2.0 pad_maximum_fusion.5
  293.2 2.0 copy.173
  295.3 15.4 %convolution_convert_fusion.1 = bf16[2048,1792]{1,0:T(8,128)(2,1)} fusion(bf16[1024,2048]{1,0:T(8,128)(2,1)} %all-gather.7.cloned.1.call-done, f32[2048]{0:T(1024)} %copy-done.35, f32[2048]{0:T(1024)S(1)} %mul.430, f32[1024]{0:T(1024)} %copy-done.38, f32[1024]{0:T(1024)} %copy-done.32, bf16[1024,1024]{1,0:T(8,128)(2,1)S(1)} %get-tuple-element.20, ...), kind=kOutput, calls=%fused_computation.14 | convolution fusion | flops 7547125760 | bytes 15228928 | tf_op jit(solution)/shard_map/dot_general | solution.py:278
  310.8 11.6 %convolution_convert_fusion.2 = bf16[1024,2048]{1,0:T(8,128)(2,1)} fusion(bf16[2048,1792]{1,0:T(8,128)(2,1)} %all-gather.9.cloned.1.call-done, bf16[1024,1024]{1,0:T(8,128)(2,1)S(1)} %get-tuple-element.20, bf16[1024,256]{1,0:T(8,128)(2,1)S(1)} %copy-done.4, bf16[1024,256]{1,0:T(8,128)(2,1)} %copy.173, bf16[1024,256]{1,0:T(8,128)(2,1)S(1)} %copy.172), kind=kOutput, calls=%fused_computation.34 | convolution fusion | flops 7532969984 | bytes 15204352 | tf_op jit(solution)/shard_map/dot_general | solution.py:285
  326.4 10.0 %convolution_convert_fusion.3 = bf16[1024,2048]{1,0:T(8,128)(2,1)} fusion(bf16[2048,1280]{1,0:T(8,128)(2,1)} %all-gather.11.cloned.1.call-done, bf16[1024,1024]{1,0:T(8,128)(2,1)} %copy-done.9, bf16[1024,256]{1,0:T(8,128)(2,1)S(1)} %copy-done.17), kind=kOutput, calls=%fused_computation.35 | convolution fusion | flops 5376049152 | bytes 12058624 | tf_op jit(solution)/shard_map/dot_general | solution.py:231
  336.5 3.6 reduce-scatter.13.cloned.1.call-done
  340.1 5.0 all_to_all.32
  345.3 80.3 %reduce-scatter.11.cloned.1.call-done = bf16[128,1792]{1,0:T(8,128)(2,1)} async-done(((bf16[2048,1792]{1,0:T(8,128)(2,1)}), bf16[128,1792]{1,0:T(8,128)(2,1)}) %reduce-scatter.11.cloned.1.call-update) | async-done | bytes 458768 | tf_op jit(solution)/shard_map/reduce_scatter | solution.py:126
  425.6 5.2 all_to_all.33
  433.4 2.0 fusion.60
  435.4 5.2 all-to-all-start.4
  440.7 2.7 convert_reduce_fusion.1
  443.5 36.1 %reduce-scatter.9.cloned.1.call-done = bf16[128,2048]{1,0:T(8,128)(2,1)} async-done(((bf16[1024,2048]{1,0:T(8,128)(2,1)}), bf16[128,2048]{1,0:T(8,128)(2,1)}) %reduce-scatter.9.cloned.1.call-update) | async-done | bytes 524304 | tf_op jit(solution)/shard_map/reduce_scatter | solution.py:288
  483.1 3.6 convolution_bitcast_fusion.1
  489.2 3.6 fusion.83
  493.3 2.1 convolution_add_fusion.3
  495.3 3.6 fusion.84
  499.4 1.9 convolution_add_fusion.2
  501.3 3.6 fusion.85
  505.3 1.9 convolution_add_fusion.1
  507.2 3.9 fusion.86
  511.5 2.8 fusion.19
  514.4 7.1 %all-to-all-start.5 = ((bf16[32,64,256]{2,1,0:T(8,128)(2,1)}), bf16[32,64,256]{2,1,0:T(8,128)(2,1)S(1)}, u32[]{:S(2)}, u32[]{:S(2)}) async-start(bf16[32,64,256]{2,1,0:T(8,128)(2,1)} %bitcast.35), calls=%async_computation.8 | async-start | bytes 2097152 | tf_op jit(solution)/shard_map/all_to_all | solution.py:359
  521.5 12.6 %reduce-scatter.7.cloned.1.call-done = bf16[128,2048]{1,0:T(8,128)(2,1)} async-done(((bf16[1024,2048]{1,0:T(8,128)(2,1)}), bf16[128,2048]{1,0:T(8,128)(2,1)}) %reduce-scatter.7.cloned.1.call-update) | async-done | bytes 524304 | tf_op jit(solution)/shard_map/reduce_scatter | solution.py:234
  534.1 3.2 convert_reduce_fusion.4
  537.4 2.3 concatenate.83
  539.7 140.5 %all-reduce.4.cloned.1.call-done = f32[11,2048]{1,0:T(8,128)} async-done(((f32[11,2048]{1,0:T(8,128)}), f32[11,2048]{1,0:T(8,128)}) %all-reduce.4.cloned.1.call-update) | async-done | bytes 90128 | tf_op jit(solution)/shard_map/psum | solution.py:325
  (245 shorter events, 51.2 us)
Async XLA Ops:
  7.2 8.9 %copy-start.10 = (f32[64,3,512]{2,0,1:T(8,128)S(1)}, f32[64,3,512]{2,0,1:T(8,128)}, u32[]{:S(2)}) copy-start(f32[64,3,512]{2,0,1:T(8,128)} %param.17) | copy-start | bytes 1179652
  7.2 9.6 %copy-start.6 = (f32[64,2048]{1,0:T(8,128)S(1)}, f32[64,2048]{1,0:T(8,128)}, u32[]{:S(2)}) copy-start(f32[64,2048]{1,0:T(8,128)} %param.19) | copy-start | bytes 1572868
  7.2 76.2 %all-gather.7.cloned.1.call-start = ((), (), s32[]{:S(2)}) async-start(), calls=%async_computation.10 | async-start | bytes 4718592 | tf_op jit(solution)/shard_map/all_gather | solution.py:154
  7.9 80.2 %all-gather.13.cloned.1.call-start = ((), (), s32[]{:S(2)}) async-start(), calls=%async_computation.14 | async-start | bytes 4718592 | tf_op jit(solution)/shard_map/all_gather | solution.py:155
  8.7 129.1 %all-gather.11.cloned.1.call-start = ((), (), s32[]{:S(2)}) async-start(), calls=%async_computation.12 | async-start | bytes 5570560 | tf_op jit(solution)/shard_map/all_gather | solution.py:122
  11.2 11.2 %copy-start.40 = (s32[512]{0:T(512)S(1)}, s32[512]{0:T(512)}, u32[]{:S(2)}) copy-start(s32[512]{0:T(512)} %param.16) | copy-start | bytes 6148
  11.2 13.0 %copy-start.29 = (f32[11,16]{1,0:T(8,128)S(1)}, f32[11,16]{1,0:T(8,128)}, u32[]{:S(2)}) copy-start(f32[11,16]{1,0:T(8,128)} %param.25) | copy-start | bytes 2116
  16.0 189.6 %all-gather.9.cloned.1.call-start = ((), (), s32[]{:S(2)}) async-start(), calls=%async_computation.11 | async-start | bytes 7798784 | tf_op jit(solution)/shard_map/all_gather | solution.py:122
  22.4 317.7 %reduce-scatter.13.cloned.1.call-start = ((), (), s32[]{:S(2)}) async-start(), calls=%async_computation.18 | async-start | bytes 5570560 | tf_op jit(solution)/shard_map/reduce_scatter | solution.py:126
  80.9 124.7 %copy-start.35 = (f32[2048]{0:T(1024)}, f32[2048]{0:T(1024)S(1)}, u32[]{:S(2)}) copy-start(f32[2048]{0:T(1024)S(1)} %add.189) | copy-start | bytes 24580
  81.6 6.4 copy-start.27
  83.4 3.4 copy-start
  86.8 118.8 %copy-start.32 = (f32[1024]{0:T(1024)}, f32[1024]{0:T(1024)S(1)}, u32[]{:S(2)}) copy-start(f32[1024]{0:T(1024)S(1)} %broadcast_multiply_fusion) | copy-start | bytes 12292
  88.1 117.6 %copy-start.38 = (f32[1024]{0:T(1024)}, f32[1024]{0:T(1024)S(1)}, u32[]{:S(2)}) copy-start(f32[1024]{0:T(1024)S(1)} %add_rsqrt_fusion) | copy-start | bytes 12292
  217.9 2.9 copy-start.3
  227.4 5.5 copy-start.12
  227.4 5.5 copy-start.14
  227.4 5.5 copy-start.22
  232.9 5.6 dynamic-slice-start
  238.5 5.7 copy-start.16
  238.5 6.9 copy-start.41
  244.2 66.6 %copy-start.2 = (bf16[1024,1024]{1,0:T(8,128)(2,1)}, bf16[1024,1024]{1,0:T(8,128)(2,1)S(1)}, u32[]{:S(2)}) copy-start(bf16[1024,1024]{1,0:T(8,128)(2,1)S(1)} %get-tuple-element.20) | copy-start | bytes 6291460
  261.3 164.3 %reduce-scatter.11.cloned.1.call-start = ((), (), s32[]{:S(2)}) async-start(), calls=%async_computation.16 | async-start | bytes 7798784 | tf_op jit(solution)/shard_map/reduce_scatter | solution.py:126
  280.8 4.9 copy-start.15
  288.1 7.2 %copy-start.4 = (bf16[1024,256]{1,0:T(8,128)(2,1)S(1)}, bf16[1024,256]{1,0:T(8,128)(2,1)}, u32[]{:S(2)}) copy-start(bf16[1024,256]{1,0:T(8,128)(2,1)} %reshape.371) | copy-start | bytes 1572868
  291.2 19.6 %copy-start.8 = (bf16[1024,256]{1,0:T(8,128)(2,1)}, bf16[1024,256]{1,0:T(8,128)(2,1)S(1)}, u32[]{:S(2)}) copy-start(bf16[1024,256]{1,0:T(8,128)(2,1)S(1)} %copy.172) | copy-start | bytes 1572868
  310.7 168.9 %reduce-scatter.9.cloned.1.call-start = ((), (), s32[]{:S(2)}) async-start(), calls=%async_computation.15 | async-start | bytes 4718592 | tf_op jit(solution)/shard_map/reduce_scatter | solution.py:288
  322.4 2.1 copy-start.25
  322.4 3.0 copy-start.20
  322.4 3.0 copy-start.21
  322.4 3.1 copy-start.1
  322.4 4.0 copy-start.17
  322.4 211.7 %reduce-scatter.7.cloned.1.call-start = ((), (), s32[]{:S(2)}) async-start(), calls=%async_computation.13 | async-start | bytes 4718592 | tf_op jit(solution)/shard_map/reduce_scatter | solution.py:234
  325.6 10.8 %copy-start.36 = (f32[128]{0:T(128)}, f32[128]{0:T(128)S(1)}, u32[]{:S(2)}) copy-start(f32[128]{0:T(128)S(1)} %broadcast_multiply_fusion.3) | copy-start | bytes 1540
  336.4 8.7 %copy-start.23 = (f32[8,2,8,256]{3,2,0,1:T(8,128)S(1)}, f32[8,2,8,256]{3,2,0,1:T(8,128)}, u32[]{:S(2)}) copy-start(f32[8,2,8,256]{3,2,0,1:T(8,128)} %copy.246) | copy-start | bytes 393220
  345.3 80.3 %copy-start.24 = (bf16[2,320,256]{2,1,0:T(8,128)(2,1)}, bf16[2,320,256]{2,1,0:T(8,128)(2,1)S(1)}, u32[]{:S(2)}) copy-start(bf16[2,320,256]{2,1,0:T(8,128)(2,1)S(1)} %slice_dynamic-update-slice_fusion) | copy-start | bytes 983044
  433.2 46.4 %copy-start.37 = (f32[128]{0:T(128)S(1)}, f32[128]{0:T(128)}, u32[]{:S(2)}) copy-start(f32[128]{0:T(128)} %copy-done.36) | copy-start | bytes 1540
  433.2 46.4 %copy-start.39 = (f32[128]{0:T(128)S(1)}, f32[128]{0:T(128)}, u32[]{:S(2)}) copy-start(f32[128]{0:T(128)} %add_rsqrt_fusion.1) | copy-start | bytes 1540
  435.4 45.8 %all-to-all-start.4 = ((bf16[32,64,256]{2,1,0:T(8,128)(2,1)}), bf16[32,64,256]{2,1,0:T(8,128)(2,1)S(1)}, u32[]{:S(2)}, u32[]{:S(2)}) async-start(bf16[32,64,256]{2,1,0:T(8,128)(2,1)} %fusion.60), calls=%async_computation.7 | async-start | bytes 2097152 | tf_op jit(solution)/shard_map/all_to_all | solution.py:357
  511.1 23.1 %copy-start.28 = (f32[2048]{0:T(1024)S(1)}, f32[2048]{0:T(1024)}, u32[]{:S(2)}) copy-start(f32[2048]{0:T(1024)} %add.207) | copy-start | bytes 24580
  511.5 168.7 %copy-start.30 = (f32[11,16]{1,0:T(8,128)S(1)}, f32[11,16]{1,0:T(8,128)}, u32[]{:S(2)}) copy-start(f32[11,16]{1,0:T(8,128)} %param.25) | copy-start | bytes 2116
  511.5 168.7 %copy-start.33 = (f32[11,16]{1,0:T(8,128)S(1)}, f32[11,16]{1,0:T(8,128)}, u32[]{:S(2)}) copy-start(f32[11,16]{1,0:T(8,128)} %param.27) | copy-start | bytes 2116
  511.5 168.7 %copy-start.34 = (f32[11,16]{1,0:T(8,128)S(1)}, f32[11,16]{1,0:T(8,128)}, u32[]{:S(2)}) copy-start(f32[11,16]{1,0:T(8,128)} %param.26) | copy-start | bytes 2116
  514.4 171.3 %all-to-all-start.5 = ((bf16[32,64,256]{2,1,0:T(8,128)(2,1)}), bf16[32,64,256]{2,1,0:T(8,128)(2,1)S(1)}, u32[]{:S(2)}, u32[]{:S(2)}) async-start(bf16[32,64,256]{2,1,0:T(8,128)(2,1)} %bitcast.35), calls=%async_computation.8 | async-start | bytes 2097152 | tf_op jit(solution)/shard_map/all_to_all | solution.py:359
  521.5 158.7 %all-reduce.4.cloned.1.call-start = ((), (), s32[]{:S(2)}) async-start(), calls=%async_computation.17 | async-start | bytes 262144 | tf_op jit(solution)/shard_map/psum | solution.py:325
  685.9 1.8 copy-start.19
  686.0 2.5 copy-start.7
  686.2 4.0 copy-start.11
  (6 other events, 7.3 us)
Sparse Core Ops, SparseCore 0:
  9.8 34.7 all-gather.6
  46.3 32.9 all-gather.12
  81.5 56.2 all-gather.10
  139.8 65.7 all-gather.8
  261.4 78.5 reduce-scatter.12
  343.4 82.1 reduce-scatter.10
  428.1 51.4 reduce-scatter.8
  482.2 51.9 reduce-scatter.6
  540.2 139.9 all-reduce.3
